TPU v7x, 32 devices: a whole 2x2x4 slice. The times are simulated.
32 devices in a mesh: pole: 4 (over y, core), row: 4 (over z), col: 2 (over x).
Axes of the slice: x: 2, y: 2, z: 4, core: 2. Of those that a mesh axis runs over, the one named last changes fastest.
Arguments:
- h_diag: float32 [8, 128, 128], P(('row', 'col'), None, 'pole'), as said below
- h_off: float32 [8, 128, 128], P(('row', 'col'), None, 'pole'), as said below
- s_diag: float32 [8, 128, 128], P(('row', 'col'), None, 'pole'), as said below
- snode_size: int32 [8], replicated, may hold values from 32 to 128, as said below
- col_order: int32 [128], replicated, may hold values from 0 to 127, as said below
- shifts: float32 [8], P('pole'), as said below
- weights: float32 [8], P('pole'), may hold values from -0.45 to 0.45, as said below
Outputs:
- density_diag: float32 [8, 128, 128], P(('row', 'col'), None, 'pole')
- density_off: float32 [8, 128, 128], P(('row', 'col'), None, 'pole')
Inputs may be any that keep to these rules, and one draw needn't show every extreme that they name: `snode_size`: rows and columns of a supernode at or beyond its live size are padding. Both ends of the range occur in every draw. `col_order`: each of 0 to 127 appears once. `h_diag`: with columns restored every block is symmetric, and for every nonnegative shift the shifted matrix is symmetric positive definite. `h_off`: couplings of the same shifted matrix. `s_diag`: with columns restored every block is symmetric positive definite. `shifts`: Positive, between 1 / 64 and 150 / 64. `weights`: magnitudes at least 0.08.
All inputs are finite; a program needn't handle non-finite values.
Results may differ from a plain program's by a relative error of at most 0.0002.
Values sent between devices are 32-bit elements; how exact they have to be, the bound alone decides.
A program may use at most 64 MiB of HBM per device.

v0:
```python
import jax
import jax.numpy as jnp
from jax import lax
from jax.sharding import PartitionSpec as P

SUPERNODE_WIDTH = 128


def shifted_2(block, axis, distance):
    devices = range(lax.axis_size(axis))
    route = [(i - distance, i) for i in devices if i - distance in devices]
    return lax.ppermute(block, axis, route)


def carried_in(part, axis, combine, identity, reverse):
    count = lax.axis_size(axis)
    place = lax.axis_index(axis)
    ahead = count - 1 - place if reverse else place
    gathered = jax.tree.map(lambda a: lax.all_gather(a, axis), part)
    state = jax.tree.map(lambda a, e: jnp.zeros_like(a) + jnp.asarray(e, a.dtype), part, identity)

    def one(turn, state):
        source = count - 1 - turn if reverse else turn
        return combine(
            state, jax.tree.map(lambda a: lax.dynamic_index_in_dim(a, source, 0, False), gathered)
        )

    return lax.fori_loop(0, ahead, one, state)


def lower_solve(factor, rhs):
    return lax.linalg.triangular_solve(factor, rhs, left_side=True, lower=True)


def upper_solve(factor, rhs):
    return lax.linalg.triangular_solve(factor, rhs, left_side=True, lower=True, transpose_a=True)


def transposed_product(left, right):
    return jnp.einsum("...ji,...jk->...ik", left, right, precision=lax.Precision.HIGHEST)


def product(left, right):
    return jnp.einsum("...ij,...jk->...ik", left, right, precision=lax.Precision.HIGHEST)


def restore(arrived, col_order):
    return jnp.zeros_like(arrived).at[:, :, col_order].set(arrived)


def compose(earlier, later):
    upper_one, cross_one, tail_one, live_one = earlier
    upper_two, cross_two, tail_two, live_two = later
    both_live = live_one * live_two
    identity_matrix = jnp.eye(upper_one.shape[-1], dtype=jnp.float32)
    pivot_block = jnp.where(both_live > 0.5, upper_two - tail_one, identity_matrix)
    factor = jnp.linalg.cholesky(pivot_block)
    left_part = lower_solve(factor, jnp.swapaxes(cross_one, -1, -2))
    right_part = lower_solve(factor, cross_two)
    joined = (
        upper_one - transposed_product(left_part, left_part),
        transposed_product(left_part, right_part),
        tail_two + transposed_product(right_part, right_part),
    )
    merged = tuple(
        (
            jnp.where(live_one < 0.5, latter, jnp.where(live_two < 0.5, former, combined))
            for former, latter, combined in zip(earlier[:3], later[:3], joined)
        )
    )
    return merged + (jnp.maximum(live_one, live_two),)


def landing(mapping):
    upper_part, cross_part, tail_part, live_part = mapping
    identity_matrix = jnp.eye(upper_part.shape[-1], dtype=jnp.float32)
    factor = jnp.linalg.cholesky(jnp.where(live_part > 0.5, upper_part, identity_matrix))
    spread = lower_solve(factor, cross_part)
    return jnp.where(live_part > 0.5, tail_part + transposed_product(spread, spread), 0.0)


def per_device(h_diag, h_off, s_diag, snode_size, col_order, shifts, weights):
    gathered = (
        lax.all_gather(h_diag, "pole", axis=2, tiled=True),
        lax.all_gather(h_off, "pole", axis=2, tiled=True),
        lax.all_gather(s_diag, "pole", axis=2, tiled=True),
    )
    hamilton, coupling_raw, intersection = (restore(section, col_order) for section in gathered)
    blocks = h_diag.shape[0]
    pole_count = shifts.shape[0]
    device_place = lax.axis_index(("row", "col"))
    widths = jnp.concatenate([snode_size, jnp.zeros((1,), jnp.int32)])
    local_widths = lax.dynamic_slice_in_dim(widths, device_place * blocks, blocks + 1)
    positions = jnp.arange(SUPERNODE_WIDTH, dtype=jnp.int32)
    live_mask = (positions[None, :] < local_widths[:, None]).astype(jnp.float32)
    diag_mask = live_mask[:-1, :, None] * live_mask[:-1, None, :]
    link_mask = live_mask[:-1, :, None] * live_mask[1:, None, :]
    coupling = coupling_raw * link_mask
    preceding = shifted_2(coupling[blocks - 1], ("row", "col"), 1)
    earlier_links = jnp.concatenate([preceding[None], coupling[:-1]], axis=0)
    identity_matrix = jnp.eye(SUPERNODE_WIDTH, dtype=jnp.float32)
    padding = identity_matrix * (1.0 - live_mask[:-1])[:, None, :]
    shifted = (hamilton[None] + shifts[:, None, None, None] * intersection[None]) * diag_mask[
        None
    ] + padding[None]
    zero_block = jnp.zeros((pole_count, SUPERNODE_WIDTH, SUPERNODE_WIDTH), jnp.float32)
    one_live = jnp.ones((), jnp.float32)

    def single_map(matrix, link):
        return (matrix, jnp.broadcast_to(link, matrix.shape), zero_block, one_live)

    forward_map = single_map(shifted[:, 0], coupling[0])
    backward_map = single_map(shifted[:, blocks - 1], jnp.swapaxes(earlier_links[blocks - 1], 0, 1))
    lone_block = jnp.zeros((1, SUPERNODE_WIDTH, SUPERNODE_WIDTH), jnp.float32)
    lone_empty = (lone_block, lone_block, lone_block, jnp.zeros((), jnp.float32))
    left_parts = []
    right_parts = []
    for pole_index in range(pole_count):
        forward_part = tuple(
            (member[pole_index : pole_index + 1] for member in forward_map[:3])
        ) + (forward_map[3],)
        backward_part = tuple(
            (member[pole_index : pole_index + 1] for member in backward_map[:3])
        ) + (backward_map[3],)
        left_parts.append(
            landing(carried_in(forward_part, ("row", "col"), compose, lone_empty, False))
        )
        right_parts.append(
            landing(carried_in(backward_part, ("row", "col"), compose, lone_empty, True))
        )
    left_state = jnp.concatenate(left_parts, axis=0)
    right_state = jnp.concatenate(right_parts, axis=0)
    carried = left_state
    block_index = 0
    left_states = [carried]
    factor = jnp.linalg.cholesky(shifted[:, block_index] - carried)
    spread = lower_solve(factor, jnp.broadcast_to(coupling[block_index], carried.shape))
    factors = factor
    carried = right_state
    right_states = [carried] * blocks
    block_index = 0
    right_states[block_index] = carried
    block_index = 0
    factor = jnp.linalg.cholesky(
        shifted[:, block_index] - left_states[block_index] - right_states[block_index]
    )
    half_inverse = lower_solve(factor, jnp.broadcast_to(identity_matrix, factor.shape))
    greens = [transposed_product(half_inverse, half_inverse)]
    following = shifted_2(greens[0], ("row", "col"), -1)
    successors = greens[1:] + [following]
    off_blocks = [-product(upper_solve(factors, spread), successors[0])]
    greens_all = jnp.stack(greens, axis=1)
    off_all = jnp.stack(off_blocks, axis=1)
    total_diag = jnp.zeros((blocks, SUPERNODE_WIDTH, SUPERNODE_WIDTH), jnp.float32)
    total_off = jnp.zeros((blocks, SUPERNODE_WIDTH, SUPERNODE_WIDTH), jnp.float32)
    for pole_index in range(pole_count):
        total_diag = total_diag + weights[pole_index] * greens_all[pole_index]
        total_off = total_off + weights[pole_index] * off_all[pole_index]
    density_diag = (total_diag * diag_mask)[:, :, col_order]
    density_off = (total_off * link_mask)[:, :, col_order]
    summed_diag, summed_off = lax.psum((density_diag, density_off), "pole")
    share_width = SUPERNODE_WIDTH // lax.axis_size("pole")
    share_start = lax.axis_index("pole") * share_width
    diag_share = lax.dynamic_slice_in_dim(summed_diag, share_start, share_width, 2)
    off_share = lax.dynamic_slice_in_dim(summed_off, share_start, share_width, 2)
    return (diag_share, off_share)


def solution(mesh):
    return jax.shard_map(
        per_device,
        mesh=mesh,
        in_specs=(
            P(("row", "col"), None, "pole"),
            P(("row", "col"), None, "pole"),
            P(("row", "col"), None, "pole"),
            P(),
            P(),
            P("pole"),
            P("pole"),
        ),
        out_specs=(P(("row", "col"), None, "pole"), P(("row", "col"), None, "pole")),
        check_vma=False,
    )
```

profile of v0, /device:TPU:0, one launch (start us, length us, event | category | flops | bytes accessed | tf_op | source)
XLA Modules:
  0.0 1168.5 jit_solution(13101587964249260713)
XLA Ops:
  34.7 31.7 %all_gather.54 = f32[8,1,128,128]{3,2,1,0:T(8,128)S(1)} all-gather(f32[1,1,128,128]{3,2,1,0:T(8,128)S(1)} %get-tuple-element.681), channel_id=1, replica_groups=mesh['pole'=4,'row'=4,'col'=2] {'row','col'}, dimensions={0}, use_global_device_ids=true | all-gather | bytes 589824 | tf_op jit(solution)/shard_map/all_gather | solution.py:19
  68.4 19.2 %all-reduce = f32[8]{0:T(128)S(1)} all-reduce(f32[8]{0:T(128)S(1)} %dynamic-update-slice.3), channel_id=1, replica_groups=mesh['pole'=4,'row'=4,'col'=2] {'row','col'}, use_global_device_ids=true, to_apply=%add | all-reduce | flops 8 | bytes 64
  87.6 31.3 %all-gather = f32[8,128,128]{2,1,0:T(8,128)S(1)} all-gather(f32[1,128,128]{2,1,0:T(8,128)S(1)} %multiply_multiply_fusion.1), channel_id=2, replica_groups=mesh['pole'=4,'row'=4,'col'=2] {'row','col'}, dimensions={0}, use_global_device_ids=true | all-gather | bytes 589824 | tf_op jit(solution)/shard_map/all_gather | solution.py:19
  119.3 11.7 %custom-call.50 = f32[1,128,128]{2,1,0:T(8,128)S(1)} custom-call(f32[1,128,128]{2,1,0:T(8,128)S(1)} %fusion.119), custom_call_target="Cholesky" | custom-call | tf_op jit(solution)/shard_map/jit(cholesky)/cholesky/custom-call.1 | solution.py:77
  131.1 214.8 %all_gather.22 = f32[8,1,128,128]{3,2,1,0:T(8,128)S(1)} all-gather(f32[1,1,128,128]{3,2,1,0:T(8,128)S(1)} %get-tuple-element.680), channel_id=1, replica_groups=mesh['pole'=4,'row'=4,'col'=2] {'row','col'}, dimensions={0}, use_global_device_ids=true | all-gather | bytes 589824 | tf_op jit(solution)/shard_map/all_gather | solution.py:19
  346.3 11.7 %custom-call.48 = f32[1,128,128]{2,1,0:T(8,128)S(1)} custom-call(f32[1,128,128]{2,1,0:T(8,128)S(1)} %fusion.123), custom_call_target="Cholesky" | custom-call | tf_op jit(solution)/shard_map/jit(cholesky)/cholesky/custom-call.1 | solution.py:77
  383.4 220.0 %all-gather.1 = f32[1024,128]{0,1:T(8,128)S(1)} all-gather(f32[128,128]{0,1:T(8,128)S(1)} %bitcast.547), channel_id=3, replica_groups=mesh['pole'=4,'row'=4,'col'=2] {'row','col'}, dimensions={0}, use_global_device_ids=true | all-gather | bytes 589824 | tf_op jit(solution)/shard_map/all_gather | solution.py:19
  603.7 188.7 %while.75 = (s32[]{:T(128)}, f32[1,128,128]{2,1,0:T(8,128)S(1)}, f32[1,128,128]{2,1,0:T(8,128)S(1)}, f32[1,128,128]{2,1,0:T(8,128)S(1)}, f32[]{:T(128)}, /*index...) while((s32[]{:T(128)}, f32[1,128,128]{2,1,0:T(8,128)S(1)}, ...), condition=%wide.region_12.15_spmd, body=%wide.region_11.14_spmd.sunk | while | flops 126156936 | bytes 1967379 | solution.py:28
  605.5 11.7 %custom-call.78 = f32[1,128,128]{2,1,0:T(8,128)S(1)} custom-call(f32[1,128,128]{2,1,0:T(8,128)S(1)} %fusion.310), custom_call_target="Cholesky" | custom-call | tf_op jit(solution)/shard_map/while/body/jit(cholesky)/cholesky/custom-call.1 | solution.py:57
  632.4 11.7 %custom-call.78 = f32[1,128,128]{2,1,0:T(8,128)S(1)} custom-call(f32[1,128,128]{2,1,0:T(8,128)S(1)} %fusion.310), custom_call_target="Cholesky" | custom-call | tf_op jit(solution)/shard_map/while/body/jit(cholesky)/cholesky/custom-call.1 | solution.py:57
  659.3 11.7 %custom-call.78 = f32[1,128,128]{2,1,0:T(8,128)S(1)} custom-call(f32[1,128,128]{2,1,0:T(8,128)S(1)} %fusion.310), custom_call_target="Cholesky" | custom-call | tf_op jit(solution)/shard_map/while/body/jit(cholesky)/cholesky/custom-call.1 | solution.py:57
  686.1 11.7 %custom-call.78 = f32[1,128,128]{2,1,0:T(8,128)S(1)} custom-call(f32[1,128,128]{2,1,0:T(8,128)S(1)} %fusion.310), custom_call_target="Cholesky" | custom-call | tf_op jit(solution)/shard_map/while/body/jit(cholesky)/cholesky/custom-call.1 | solution.py:57
  713.0 11.7 %custom-call.78 = f32[1,128,128]{2,1,0:T(8,128)S(1)} custom-call(f32[1,128,128]{2,1,0:T(8,128)S(1)} %fusion.310), custom_call_target="Cholesky" | custom-call | tf_op jit(solution)/shard_map/while/body/jit(cholesky)/cholesky/custom-call.1 | solution.py:57
  739.9 11.7 %custom-call.78 = f32[1,128,128]{2,1,0:T(8,128)S(1)} custom-call(f32[1,128,128]{2,1,0:T(8,128)S(1)} %fusion.310), custom_call_target="Cholesky" | custom-call | tf_op jit(solution)/shard_map/while/body/jit(cholesky)/cholesky/custom-call.1 | solution.py:57
  766.8 11.7 %custom-call.78 = f32[1,128,128]{2,1,0:T(8,128)S(1)} custom-call(f32[1,128,128]{2,1,0:T(8,128)S(1)} %fusion.310), custom_call_target="Cholesky" | custom-call | tf_op jit(solution)/shard_map/while/body/jit(cholesky)/cholesky/custom-call.1 | solution.py:57
  792.6 11.7 %custom-call.54 = f32[1,128,128]{2,1,0:T(8,128)S(1)} custom-call(f32[1,128,128]{2,1,0:T(8,128)S(1)} %copy.170), custom_call_target="Cholesky" | custom-call | tf_op jit(solution)/shard_map/jit(cholesky)/cholesky/custom-call.1 | solution.py:77
  804.5 189.2 %while.74 = (s32[]{:T(128)}, f32[1,128,128]{2,1,0:T(8,128)S(1)}, f32[1,128,128]{2,1,0:T(8,128)S(1)}, f32[1,128,128]{2,1,0:T(8,128)S(1)}, f32[]{:T(128)}, /*index...) while((s32[]{:T(128)}, f32[1,128,128]{2,1,0:T(8,128)S(1)}, ...), condition=%wide.region_10.13_spmd, body=%wide.region_9.12_spmd.sunk | while | flops 126156936 | bytes 1967379 | solution.py:28
  806.1 11.7 %custom-call.76 = f32[1,128,128]{2,1,0:T(8,128)S(1)} custom-call(f32[1,128,128]{2,1,0:T(8,128)S(1)} %fusion.292), custom_call_target="Cholesky" | custom-call | tf_op jit(solution)/shard_map/while/body/jit(cholesky)/cholesky/custom-call.1 | solution.py:57
  833.0 11.7 %custom-call.76 = f32[1,128,128]{2,1,0:T(8,128)S(1)} custom-call(f32[1,128,128]{2,1,0:T(8,128)S(1)} %fusion.292), custom_call_target="Cholesky" | custom-call | tf_op jit(solution)/shard_map/while/body/jit(cholesky)/cholesky/custom-call.1 | solution.py:57
  860.0 11.7 %custom-call.76 = f32[1,128,128]{2,1,0:T(8,128)S(1)} custom-call(f32[1,128,128]{2,1,0:T(8,128)S(1)} %fusion.292), custom_call_target="Cholesky" | custom-call | tf_op jit(solution)/shard_map/while/body/jit(cholesky)/cholesky/custom-call.1 | solution.py:57
  872.9 9.8 custom-call.77
  887.0 11.7 %custom-call.76 = f32[1,128,128]{2,1,0:T(8,128)S(1)} custom-call(f32[1,128,128]{2,1,0:T(8,128)S(1)} %fusion.292), custom_call_target="Cholesky" | custom-call | tf_op jit(solution)/shard_map/while/body/jit(cholesky)/cholesky/custom-call.1 | solution.py:57
  913.9 11.7 %custom-call.76 = f32[1,128,128]{2,1,0:T(8,128)S(1)} custom-call(f32[1,128,128]{2,1,0:T(8,128)S(1)} %fusion.292), custom_call_target="Cholesky" | custom-call | tf_op jit(solution)/shard_map/while/body/jit(cholesky)/cholesky/custom-call.1 | solution.py:57
  940.9 11.7 %custom-call.76 = f32[1,128,128]{2,1,0:T(8,128)S(1)} custom-call(f32[1,128,128]{2,1,0:T(8,128)S(1)} %fusion.292), custom_call_target="Cholesky" | custom-call | tf_op jit(solution)/shard_map/while/body/jit(cholesky)/cholesky/custom-call.1 | solution.py:57
  967.9 11.7 %custom-call.76 = f32[1,128,128]{2,1,0:T(8,128)S(1)} custom-call(f32[1,128,128]{2,1,0:T(8,128)S(1)} %fusion.292), custom_call_target="Cholesky" | custom-call | tf_op jit(solution)/shard_map/while/body/jit(cholesky)/cholesky/custom-call.1 | solution.py:57
  980.8 9.8 custom-call.77
  994.0 11.7 %custom-call.52 = f32[1,128,128]{2,1,0:T(8,128)S(1)} custom-call(f32[1,128,128]{2,1,0:T(8,128)S(1)} %copy.160), custom_call_target="Cholesky" | custom-call | tf_op jit(solution)/shard_map/jit(cholesky)/cholesky/custom-call.1 | solution.py:77
  1029.9 23.7 %custom-call.58 = f32[2,128,128]{2,1,0:T(8,128)S(1)} custom-call(f32[2,128,128]{2,1,0:T(8,128)S(1)} %fusion.88), custom_call_target="Cholesky" | custom-call | tf_op jit(solution)/shard_map/jit(cholesky)/cholesky | solution.py:136
  1053.7 23.5 %custom-call.56 = f32[2,128,128]{2,1,0:T(8,128)S(1)} custom-call(f32[2,128,128]{2,1,0:T(8,128)S(1)} %fusion.91), custom_call_target="Cholesky" | custom-call | tf_op jit(solution)/shard_map/jit(cholesky)/cholesky | solution.py:144
  1077.6 19.7 %custom-call.15 = f32[2,1,128,128]{2,3,1,0:T(8,128)S(1)} custom-call(f32[2,1,128,128]{3,2,1,0:T(8,128)S(1)} %get-tuple-element.682), custom_call_target="InvertDiagBlocksLowerTriangular" | custom-call | tf_op jit(solution)/shard_map/triangular_solve | solution.py:36
  1097.6 20.0 %custom-call.57 = f32[2,1,128,128]{2,3,1,0:T(8,128)S(1)} custom-call(f32[2,1,128,128]{3,2,1,0:T(8,128)S(1)} %get-tuple-element.683), custom_call_target="InvertDiagBlocksLowerTriangular" | custom-call | tf_op jit(solution)/shard_map/triangular_solve/custom-call.3 | solution.py:32
  1129.6 28.9 %all-reduce.4.cloned.1.call-done = (f32[1,128,128]{1,2,0:T(8,128)}, f32[1,128,128]{1,2,0:T(8,128)}) async-done(((f32[1,128,128]{1,2,0:T(8,128)}, f32[1,128,128]{1,2,0:T(8,128)}), (f32[1,128,128]{1,2,0:T(8,128)}, f32[1,128,128]{1,2,0:T(8,128)})) %all-reduce.4.cloned.1.call-update) | async-done | bytes 131088 | tf_op jit(solution)/shard_map/psum | solution.py:161
  (321 shorter events, 261.1 us)
Async XLA Ops:
  7.2 1.6 copy-start
  7.2 1151.3 %all-reduce.4.cloned.1.call-start = ((), (), s32[]{:S(2)}) async-start(), calls=%async_computation | async-start | bytes 262144 | tf_op jit(solution)/shard_map/psum | solution.py:161
  7.2 0.7 copy-start.5
  8.1 0.7 copy-start.6
  16.0 367.4 %collective-permute-start = (f32[128,128]{1,0:T(8,128)S(1)}, f32[128,128]{1,0:T(8,128)S(1)}, u32[]{:S(2)}, u32[]{:S(2)}) collective-permute-start(f32[128,128]{1,0:T(8,128)S(1)} %fusion.172), channel_id=1, source_target_pairs={{0,1},{1,2},{2,3},{3,4},{4,5},{5,6},{6,7},{8,9},{9,10},{10,11},{11... | collective-permute-start | bytes 196616 | tf_op jit(solution)/shard_map/ppermute | solution.py:12
  20.3 0.7 copy-start.1
  27.1 0.7 copy-start.2
  34.0 0.7 copy-start.4
  66.4 0.7 copy-start.7
  382.1 0.7 copy-start.3
  1118.4 6.9 collective-permute-start.1
Sparse Core Ops, SparseCore 0:
  1129.7 28.7 all-reduce.3
where the time goes:
time: 1180 us; the launch traced here: 1170 us
  blocking collectives  534 us (45%)
  other arithmetic  500 us (42%)
  waiting for transfers between devices  34.2 us (3%)
  loops' own time  29.4 us (2%)
  local copies, waits for them, and re-layouts  26.5 us (2%)
  matrix products  24.2 us (2%)
  between operations  15.3 us (1%)
    all_gather x4, blocking collectives, carried_in(): gathered = jax.tree.map(lambda a: lax.all_gather(a, axis), part)  498 us
    another operation x38, other arithmetic, lower_solve(): return lax.linalg.triangular_solve(factor, rhs, left_side=True, lower=True)  207 us
    another operation x42, other arithmetic, compose(): factor = jnp.linalg.cholesky(pivot_block)  173 us
    another operation x12, other arithmetic, landing(): jnp.linalg.cholesky(jnp.where(live_part > 0.5, upper_part, identity_matrix))  49.7 us
    another operation x4, loops' own time, carried_in(): return lax.fori_loop(0, ahead, one, state)  29.4 us
    psum x1, waiting for transfers between devices, per_device(): summed_diag, summed_off = lax.psum((density_diag, density_off), 'pole')  28.9 us
    another operation x3, other arithmetic, per_device(): factor = jnp.linalg.cholesky(shifted[:, block_index] - carried)  23.9 us
  transfers between devices with their start and end apart: 3, of which 2 were waited for; matrix products, arithmetic and copies ran while one was open for 4% of the time, Pallas kernels for 0%

commit v1 on v0

v1 whole, which is shorter than its diff:
```python
import functools

import jax
import jax.numpy as jnp
from jax import lax
from jax.experimental import pallas as pl
from jax.experimental.pallas import tpu as pltpu
from jax.sharding import PartitionSpec as P

MESH = pl.DeviceIdType.MESH
N = 128
PANEL = 8


def dot(a, b):
    return lax.dot_general(
        a, b, (((1,), (0,)), ((), ())), precision=lax.Precision.HIGHEST,
        preferred_element_type=jnp.float32,
    )


def dot_t(a, b):
    return lax.dot_general(
        a, b, (((1,), (1,)), ((), ())), precision=lax.Precision.HIGHEST,
        preferred_element_type=jnp.float32,
    )


def lane(x, index):
    return jnp.take_along_axis(x, jnp.full(x.shape, index, jnp.int32), axis=1)


def invert(work, members):
    sub = lax.broadcasted_iota(jnp.int32, (PANEL, N), 0)
    lanes = lax.broadcasted_iota(jnp.int32, (PANEL, N), 1)

    def step(k, _):
        base = pl.multiple_of(k * PANEL, PANEL)
        inside = (lanes >= base) & (lanes < base + PANEL)
        for m in members:
            rows = work[m, pl.ds(base, PANEL), :]
            cols = [lane(rows, base + j) for j in range(PANEL)]
            rows = jnp.where(inside, jnp.where(lanes - base == sub, 1.0, 0.0), rows)
            for j in range(PANEL):
                pivot = sub == j
                r = 1.0 / jnp.broadcast_to(cols[j][j : j + 1], (PANEL, N))
                f = cols[j]

                def swept(x):
                    top = jnp.broadcast_to(x[j : j + 1], (PANEL, N))
                    return jnp.where(pivot, 0.0, x) - jnp.where(pivot, -top, f * top) * r

                cols = cols[: j + 1] + [swept(c) for c in cols[j + 1 :]]
                rows = swept(rows)
            tops = [jnp.broadcast_to(rows[j : j + 1], (PANEL, N)) for j in range(PANEL)]
            for t in range(N // PANEL):
                x = work[m, t * PANEL : (t + 1) * PANEL, :]
                parts = [lane(x, base + j) * tops[j] for j in range(PANEL)]
                while len(parts) > 1:
                    parts = [a + b for a, b in zip(parts[::2], parts[1::2])]
                work[m, t * PANEL : (t + 1) * PANEL, :] = jnp.where(inside, 0.0, x) - parts[0]
            work[m, pl.ds(base, PANEL), :] = rows
        return 0

    lax.fori_loop(0, N // PANEL, step, 0)


def kernel(
    n_pole, n_col, places, poles, levels,
    h_ref, o_ref, s_ref, size_ref, order_ref, shift_ref, weight_ref,
    diag_ref, off_ref,
    mixed, gathered, coupling_t, link_t, a_all, work, f_all, ul,
    send_l, send_r, recv_l, recv_r, g_send, g_recv, z_send, z_recv,
    gs, gr, cs, cr, ls, lr, rs, rr, ns, nr, zs, zr,
):
    q = lax.axis_index("pole")
    place = lax.axis_index("row") * n_col + lax.axis_index("col")
    share = N // n_pole

    def at(target):
        return {"row": target // n_col, "col": lax.rem(target, n_col)}

    def mate(o):
        return {"pole": lax.rem(q + o, n_pole)}

    distances = [1 << l for l in range(levels)]
    barrier = pltpu.get_barrier_semaphore()
    for o in range(1, n_pole):
        pl.semaphore_signal(barrier, inc=1, device_id=mate(o), device_id_type=MESH)
    count = n_pole - 1
    for d in distances:
        has_right = place + d < places
        has_left = place >= d

        @pl.when(has_right)
        def _():
            pl.semaphore_signal(barrier, inc=1, device_id=at(place + d), device_id_type=MESH)

        @pl.when(has_left)
        def _():
            pl.semaphore_signal(barrier, inc=1, device_id=at(place - d), device_id_type=MESH)

        count = count + has_right.astype(jnp.int32) + has_left.astype(jnp.int32)

    mixed[...] = jnp.zeros_like(mixed)
    mixed[:, 0:share] = h_ref[0]
    mixed[:, share : 2 * share] = o_ref[0]
    mixed[:, 2 * share : 3 * share] = s_ref[0]
    turned = mixed[...].T
    mine = pl.ds(pl.multiple_of(q * share, share), share)
    for i in range(3):
        gathered[mine, i * N : (i + 1) * N] = turned[i * share : (i + 1) * share]
    pl.semaphore_wait(barrier, count)
    copies = []
    for o in range(1, n_pole):
        copy = pltpu.make_async_remote_copy(
            src_ref=gathered.at[mine], dst_ref=gathered.at[mine],
            send_sem=gs.at[o - 1], recv_sem=gr.at[o - 1],
            device_id=mate(o), device_id_type=MESH,
        )
        copy.start()
        copies.append(copy)

    iota0 = lax.broadcasted_iota(jnp.int32, (N, N), 0)
    iota1 = lax.broadcasted_iota(jnp.int32, (N, N), 1)
    one_hot = jnp.where(iota0 == order_ref[...], 1.0, 0.0)
    size = size_ref[place]
    after = size_ref[jnp.minimum(place + 1, places - 1)]
    after = jnp.where(place + 1 < places, after, 0)
    diag_mask = (iota0 < size) & (iota1 < size)
    link_mask_t = (iota0 < after) & (iota1 < size)
    padding = jnp.where((iota0 == iota1) & (iota1 >= size), 1.0, 0.0)

    for copy in copies:
        copy.wait()
    restored = dot(one_hot, gathered[...])
    coupling_t[...] = jnp.where(link_mask_t, restored[:, N : 2 * N], 0.0)

    has_right = place + 1 < places
    has_left = place >= 1
    to_right = pltpu.make_async_remote_copy(
        src_ref=coupling_t, dst_ref=link_t, send_sem=cs, recv_sem=cr,
        device_id=at(jnp.minimum(place + 1, places - 1)), device_id_type=MESH,
    )

    @pl.when(has_right)
    def _():
        to_right.start()

    for p in range(poles):
        a = restored[:, :N] + shift_ref[p] * restored[:, 2 * N :]
        a = jnp.where(diag_mask, a, 0.0) + padding
        a_all[p] = a
        work[p] = a
        f_all[p] = jnp.zeros((N, N), jnp.float32)

    for level, d in enumerate(distances):
        last = level == levels - 1
        half = N if last else 2 * N
        invert(work, range(poles))
        if level == 0:
            @pl.when(has_left)
            def _():
                to_right.wait_recv()

            @pl.when(jnp.logical_not(has_left))
            def _():
                link_t[...] = jnp.zeros_like(link_t)

            for p in range(poles):
                ul[p, :N] = coupling_t[...]
                ul[p, N:] = link_t[...].T
        has_right_d = place + d < places
        has_left_d = place >= d
        rights, lefts = [], []
        for p in range(poles):
            if level:
                ul[p, :N] = recv_r[level - 1, p, :N]
                ul[p, N:] = recv_l[level - 1, p, N:]
            both = ul[p]
            product = dot(both, work[p])
            full = dot_t(product, both)
            send_r[level, p] = full[:, :N]
            send_l[level, p] = full[:, N:]
            right = pltpu.make_async_remote_copy(
                src_ref=send_r.at[level, p, pl.ds(0, half)],
                dst_ref=recv_l.at[level, p, pl.ds(0, half)],
                send_sem=rs.at[level, p], recv_sem=rr.at[level, p],
                device_id=at(jnp.minimum(place + d, places - 1)), device_id_type=MESH,
            )
            low = 2 * N - half
            left = pltpu.make_async_remote_copy(
                src_ref=send_l.at[level, p, pl.ds(low, half)],
                dst_ref=recv_r.at[level, p, pl.ds(low, half)],
                send_sem=ls.at[level, p], recv_sem=lr.at[level, p],
                device_id=at(jnp.maximum(place - d, 0)), device_id_type=MESH,
            )
            rights.append(right)
            lefts.append(left)

            @pl.when(has_right_d)
            def _():
                right.start()

            @pl.when(has_left_d)
            def _():
                left.start()

        @pl.when(jnp.logical_not(has_left_d))
        def _():
            recv_l[level] = jnp.zeros(recv_l.shape[1:], jnp.float32)

        @pl.when(jnp.logical_not(has_right_d))
        def _():
            recv_r[level] = jnp.zeros(recv_r.shape[1:], jnp.float32)

        for p in range(poles):
            @pl.when(has_left_d)
            def _():
                rights[p].wait_recv()

            @pl.when(has_right_d)
            def _():
                lefts[p].wait_recv()

            @pl.when(has_right_d)
            def _():
                rights[p].wait_send()

            @pl.when(has_left_d)
            def _():
                lefts[p].wait_send()

        for p in range(poles):
            f_all[p] += recv_l[level, p, :N]
            e = jnp.zeros((N, N), jnp.float32)
            for earlier in range(level + 1):
                e += recv_r[earlier, p, N:]
            work[p] = a_all[p] - f_all[p] - e

    @pl.when(has_right)
    def _():
        to_right.wait_send()

    for p in range(poles):
        work[poles + p] = a_all[p] - f_all[p]
    invert(work, range(2 * poles))

    total = jnp.zeros((N, N), jnp.float32)
    for p in range(poles):
        scaled = weight_ref[p] * work[p]
        g_send[p] = scaled
        total += scaled
    to_left = pltpu.make_async_remote_copy(
        src_ref=g_send, dst_ref=g_recv, send_sem=ns, recv_sem=nr,
        device_id=at(jnp.maximum(place - 1, 0)), device_id_type=MESH,
    )

    @pl.when(has_left)
    def _():
        to_left.start()

    halves = [dot(coupling_t[...], work[poles + p]) for p in range(poles)]
    order = one_hot.T
    z_send[:, :N] = dot(order, jnp.where(diag_mask, total, 0.0))

    @pl.when(has_right)
    def _():
        to_left.wait_recv()

    @pl.when(jnp.logical_not(has_right))
    def _():
        g_recv[...] = jnp.zeros_like(g_recv)

    off_t = jnp.zeros((N, N), jnp.float32)
    for p in range(poles):
        off_t -= dot(g_recv[p], halves[p])
    z_send[:, N:] = dot(order, jnp.where(link_mask_t, off_t, 0.0))

    copies = []
    for o in range(1, n_pole):
        theirs = pl.ds(pl.multiple_of(lax.rem(q + o, n_pole) * share, share), share)
        copy = pltpu.make_async_remote_copy(
            src_ref=z_send.at[theirs], dst_ref=z_recv.at[o - 1],
            send_sem=zs.at[o - 1], recv_sem=zr.at[o - 1],
            device_id=mate(o), device_id_type=MESH,
        )
        copy.start()
        copies.append(copy)

    @pl.when(has_left)
    def _():
        to_left.wait_send()

    result = z_send[mine]
    for o in range(1, n_pole):
        copies[o - 1].wait()
        result += z_recv[o - 1]
    mixed[0:share] = result[:, :N]
    mixed[share : 2 * share] = result[:, N:]
    turned = mixed[...].T
    diag_ref[0] = turned[:, :share]
    off_ref[0] = turned[:, share : 2 * share]


def solution(mesh):
    n_pole, n_row, n_col = (mesh.shape[a] for a in ("pole", "row", "col"))
    places = n_row * n_col
    levels = (places - 1).bit_length()

    def per_device(h_diag, h_off, s_diag, snode_size, col_order, shifts, weights):
        poles = shifts.shape[0]
        share = h_diag.shape[2]
        vmem = pl.BlockSpec(memory_space=pltpu.VMEM)
        smem = pl.BlockSpec(memory_space=pltpu.SMEM)
        f32 = functools.partial(lambda *shape: pltpu.VMEM(shape, jnp.float32))
        dma = pltpu.SemaphoreType.DMA
        message = f32(levels, poles, 2 * N, N)
        return tuple(
            pl.pallas_call(
                functools.partial(kernel, n_pole, n_col, places, poles, levels),
                out_shape=[jax.ShapeDtypeStruct((1, N, share), jnp.float32)] * 2,
                in_specs=[vmem, vmem, vmem, smem, vmem, smem, smem],
                out_specs=[vmem, vmem],
                scratch_shapes=[
                    f32(N, N), f32(N, 3 * N), f32(N, N), f32(N, N), f32(poles, N, N),
                    f32(2 * poles, N, N), f32(poles, N, N), f32(poles, 2 * N, N),
                    message, message, message, message,
                    f32(poles, N, N), f32(poles, N, N), f32(N, 2 * N),
                    f32(n_pole - 1, share, 2 * N),
                    dma((n_pole - 1,)), dma((n_pole - 1,)), dma, dma,
                    dma((levels, poles)), dma((levels, poles)),
                    dma((levels, poles)), dma((levels, poles)),
                    dma, dma, dma((n_pole - 1,)), dma((n_pole - 1,)),
                ],
                compiler_params=pltpu.CompilerParams(
                    collective_id=0, has_side_effects=True,
                    vmem_limit_bytes=32 * 1024 * 1024,
                ),
            )(h_diag, h_off, s_diag, snode_size, col_order.reshape(1, N), shifts, weights)
        )

    spread = P(("row", "col"), None, "pole")
    return jax.shard_map(
        per_device,
        mesh=mesh,
        in_specs=(spread, spread, spread, P(), P(), P("pole"), P("pole")),
        out_specs=(spread, spread),
        check_vma=False,
    )
```

time: 1180 us -> 124 us (0.11)
  blocking collectives: 534 us -> 0 us
  other arithmetic: 500 us -> 0 us
  Pallas kernels: 0 us -> 120 us
  waiting for transfers between devices: 34.2 us -> 0 us
  loops' own time: 29.4 us -> 0 us
  matrix products: 24.2 us -> 0 us
  local copies, waits for them, and re-layouts: 26.5 us -> 3.59 us
  between operations: 15.3 us -> 0.67 us
    all_gather x7 -> x0, blocking collectives: 514 us -> none  [the longest x4 498 us: carried_in(): gathered = jax.tree.map(lambda a: lax.all_gather(a, axis), part)]
    another operation x100 -> x0, other arithmetic: 497 us -> none  [the longest x38 207 us: lower_solve(): return lax.linalg.triangular_solve(factor, rhs, left_side=True, lower=True)]
    pallas_call x0 -> x1, Pallas kernels: none -> 120 us  [per_device(): pl.pallas_call(functools.partial(kernel, n_pole, n_col, places, poles, le...]
    another operation x4 -> x0, loops' own time: 29.4 us -> none  [carried_in(): return lax.fori_loop(0, ahead, one, state)]
    psum x1 -> x0, waiting for transfers between devices: 28.9 us -> none  [per_device(): summed_diag, summed_off = lax.psum((density_diag, density_off), 'pole')]
    unnamed x1 -> x0, blocking collectives: 19.2 us -> none
    dot_general x48 -> x0, matrix products: 14 us -> none  [the longest x47 13.8 us: transposed_product(): jnp.einsum('...ji,...jk->...ik', left, right, precision=lax.Precision.HIG...]
  transfers between devices with their start and end apart: 3 -> 0, of which waited for: 2 -> 0; matrix products, arithmetic and copies ran while one was open for 4% -> 0% of each run, Pallas kernels for 0% -> 0%
where the time goes in v1:
time: 124 us
  Pallas kernels  120 us (97%)
  local copies, waits for them, and re-layouts  3.59 us (3%)
    pallas_call x1, Pallas kernels, per_device(): pl.pallas_call(functools.partial(kernel, n_pole, n_col, places, poles, le...  120 us

profile of v1, /device:TPU:0, one launch (start us, length us, event | category | flops | bytes accessed | tf_op | source)
XLA Modules:
  0.0 124.1 jit_solution(14818533105516510362)
XLA Ops:
  0.6 0.0 copy-start.4
  0.6 0.8 copy.9.h_ref
  1.5 0.0 copy-done.4
  1.5 0.0 copy-start.5
  1.5 0.1 copy.10.o_ref
  1.6 0.6 copy-done.5
  2.2 0.0 copy-start
  2.2 0.0 copy-start.1
  2.2 0.0 copy-start.2
  2.2 0.0 copy-start.3
  2.2 0.1 copy.11.s_ref
  2.3 0.5 copy-done
  2.8 0.0 copy-done.1
  2.9 0.0 copy-done.2
  2.9 0.0 copy-done.3
  2.9 119.8 %shard_map.86 = (f32[1,128,32]{2,1,0:T(8,128)S(1)}, f32[1,128,32]{2,1,0:T(8,128)S(1)}) custom-call(f32[1,128,32]{2,1,0:T(8,128)S(1)} %copy.9.h_ref, f32[1,128,32]{2,1,0:T(8,128)S(1)} %copy.10.o_ref, f32[1,128,32]{2,1,0:T(8,128)S(1)} %copy.11.s_ref, s32[8]{0:T(128)S(1)} %copy-done, s32[1,128]{1,0:T(1,128)S(1)} %bitcast.1, f32[2]{0:T(128)S(1)} %copy-done.2, ...), custom_call_target="tpu_custom_call" | custom-call | tf_op jit(solution)/shard_map/pallas_call | solution.py:320
  122.7 0.7 copy.12
  123.4 0.7 copy.13
Async XLA Ops:
  0.6 0.8 copy-start.4
  1.5 0.7 copy-start.5
  2.2 0.7 copy-start
  2.2 0.7 copy-start.1
  2.2 0.7 copy-start.2
  2.2 0.7 copy-start.3

commit v2 on v1

--- a/solution.py
+++ b/solution.py
@@ -9,7 +9,7 @@
 
 MESH = pl.DeviceIdType.MESH
 N = 128
-PANEL = 8
+PANEL = 16
 
 
 def dot(a, b):
@@ -30,36 +30,60 @@
     return jnp.take_along_axis(x, jnp.full(x.shape, index, jnp.int32), axis=1)
 
 
+def reciprocal(x):
+    r = pl.reciprocal(x, approx=True)
+    r = r * (2.0 - x * r)
+    return r * (2.0 - x * r)
+
+
+def eliminate(rows, cols, sub):
+    shape = (PANEL, N)
+    members = range(len(rows))
+    for j in range(PANEL):
+        pivot = sub == j
+        tops = [
+            [jnp.broadcast_to(cols[m][i][j : j + 1], shape) for i in range(j, PANEL)]
+            for m in members
+        ]
+        scale = [
+            jnp.concatenate([reciprocal(tops[m][0][:8])] * (PANEL // 8), axis=0) for m in members
+        ]
+        ends = [jnp.broadcast_to(rows[m][j : j + 1], shape) for m in members]
+        fs = [jnp.where(pivot, -1.0, cols[m][j]) for m in members]
+        for i in range(j + 1, PANEL):
+            for m in members:
+                cols[m][i] = (
+                    jnp.where(pivot, 0.0, cols[m][i]) - (fs[m] * tops[m][i - j]) * scale[m]
+                )
+        for m in members:
+            rows[m] = jnp.where(pivot, 0.0, rows[m]) - (fs[m] * ends[m]) * scale[m]
+    return rows
+
+
 def invert(work, members):
     sub = lax.broadcasted_iota(jnp.int32, (PANEL, N), 0)
     lanes = lax.broadcasted_iota(jnp.int32, (PANEL, N), 1)
+    all_subs = lax.broadcasted_iota(jnp.int32, (N, N), 0)
+    all_lanes = lax.broadcasted_iota(jnp.int32, (N, N), 1)
 
     def step(k, _):
         base = pl.multiple_of(k * PANEL, PANEL)
+        rows = [work[m, pl.ds(base, PANEL), :] for m in members]
         inside = (lanes >= base) & (lanes < base + PANEL)
-        for m in members:
-            rows = work[m, pl.ds(base, PANEL), :]
-            cols = [lane(rows, base + j) for j in range(PANEL)]
-            rows = jnp.where(inside, jnp.where(lanes - base == sub, 1.0, 0.0), rows)
-            for j in range(PANEL):
-                pivot = sub == j
-                r = 1.0 / jnp.broadcast_to(cols[j][j : j + 1], (PANEL, N))
-                f = cols[j]
-
-                def swept(x):
-                    top = jnp.broadcast_to(x[j : j + 1], (PANEL, N))
-                    return jnp.where(pivot, 0.0, x) - jnp.where(pivot, -top, f * top) * r
-
-                cols = cols[: j + 1] + [swept(c) for c in cols[j + 1 :]]
-                rows = swept(rows)
-            tops = [jnp.broadcast_to(rows[j : j + 1], (PANEL, N)) for j in range(PANEL)]
-            for t in range(N // PANEL):
-                x = work[m, t * PANEL : (t + 1) * PANEL, :]
-                parts = [lane(x, base + j) * tops[j] for j in range(PANEL)]
-                while len(parts) > 1:
-                    parts = [a + b for a, b in zip(parts[::2], parts[1::2])]
-                work[m, t * PANEL : (t + 1) * PANEL, :] = jnp.where(inside, 0.0, x) - parts[0]
-            work[m, pl.ds(base, PANEL), :] = rows
+        cols = [[lane(r, base + j) for j in range(PANEL)] for r in rows]
+        unit = jnp.where(lanes - base == sub, 1.0, 0.0)
+        done = eliminate([jnp.where(inside, unit, r) for r in rows], cols, sub)
+        panel_lanes = (all_lanes >= base) & (all_lanes < base + PANEL)
+        panel_subs = (all_subs >= base) & (all_subs < base + PANEL)
+        outs = []
+        for i, m in enumerate(members):
+            x = work[m]
+            tall = jnp.concatenate([done[i]] * (N // PANEL), axis=0)
+            left = jnp.where(panel_lanes, x, 0.0)
+            rest = x - left - dot(left, jnp.where(panel_subs, tall, 0.0))
+            outs.append(jnp.where(panel_subs, tall, rest))
+        for i, m in enumerate(members):
+            work[m] = outs[i]
         return 0
 
     lax.fori_loop(0, N // PANEL, step, 0)

time: 124 us -> 78.8 us (0.64)
  Pallas kernels: 120 us -> 74.2 us
    pallas_call x1, Pallas kernels: 120 us -> 74.2 us  [per_device(): pl.pallas_call(functools.partial(kernel, n_pole, n_col, places, poles, le...]
where the time goes in v2:
time: 78.8 us; the launch traced here: 78.4 us
  Pallas kernels  74.2 us (94%)
  local copies, waits for them, and re-layouts  3.59 us (5%)
    pallas_call x1, Pallas kernels, per_device(): pl.pallas_call(functools.partial(kernel, n_pole, n_col, places, poles, le...  74.2 us
    unnamed x15, local copies, waits for them, and re-layouts  2.23 us

profile of v2, /device:TPU:0, one launch (start us, length us, event | category | flops | bytes accessed | tf_op | source)
XLA Modules:
  0.0 78.4 jit_solution(3553604697479371836)
XLA Ops:
  0.6 0.0 copy-start.4
  0.6 0.8 %copy.9.h_ref = f32[1,128,32]{2,1,0:T(8,128)S(1)} copy(f32[1,128,32]{1,2,0:T(8,128)} %param.7) | data formatting | bytes 32768 | tf_op args[0]
  1.5 0.0 copy-done.4
  1.5 0.0 copy-start.5
  1.5 0.1 copy.10.o_ref
  1.6 0.6 copy-done.5
  2.2 0.0 copy-start
  2.2 0.0 copy-start.1
  2.2 0.0 copy-start.2
  2.2 0.0 copy-start.3
  2.2 0.1 copy.11.s_ref
  2.3 0.5 copy-done
  2.8 0.0 copy-done.1
  2.9 0.0 copy-done.2
  2.9 0.0 copy-done.3
  2.9 74.2 %shard_map.86 = (f32[1,128,32]{2,1,0:T(8,128)S(1)}, f32[1,128,32]{2,1,0:T(8,128)S(1)}) custom-call(f32[1,128,32]{2,1,0:T(8,128)S(1)} %copy.9.h_ref, f32[1,128,32]{2,1,0:T(8,128)S(1)} %copy.10.o_ref, f32[1,128,32]{2,1,0:T(8,128)S(1)} %copy.11.s_ref, s32[8]{0:T(128)S(1)} %copy-done, s32[1,128]{1,0:T(1,128)S(1)} %bitcast.1, f32[2]{0:T(128)S(1)} %copy-done.2, ...), custom_call_target="tpu_custom_call" | custom-call | tf_op jit(solution)/shard_map/pallas_call | solution.py:344
  77.1 0.7 copy.12
  77.8 0.7 copy.13
Async XLA Ops:
  0.6 0.8 %copy-start.4 = (f32[1,128,32]{1,2,0:T(8,128)S(1)}, f32[1,128,32]{1,2,0:T(8,128)}, u32[]{:S(2)}) copy-start(f32[1,128,32]{1,2,0:T(8,128)} %param.8) | copy-start | bytes 49156
  1.5 0.7 copy-start.5
  2.2 0.7 copy-start
  2.2 0.7 copy-start.1
  2.2 0.7 copy-start.2
  2.2 0.7 copy-start.3

commit v3 on v2

--- a/solution.py
+++ b/solution.py
@@ -32,7 +32,6 @@
 
 def reciprocal(x):
     r = pl.reciprocal(x, approx=True)
-    r = r * (2.0 - x * r)
     return r * (2.0 - x * r)
 
 
@@ -93,9 +92,9 @@
     n_pole, n_col, places, poles, levels,
     h_ref, o_ref, s_ref, size_ref, order_ref, shift_ref, weight_ref,
     diag_ref, off_ref,
-    mixed, gathered, coupling_t, link_t, a_all, work, f_all, ul,
-    send_l, send_r, recv_l, recv_r, g_send, g_recv, z_send, z_recv,
-    gs, gr, cs, cr, ls, lr, rs, rr, ns, nr, zs, zr,
+    gathered, coupling_t, link_t, a_all, work, f_all, d_all, ul,
+    t_send, t_recv, n_send, n_recv, g_send, g_recv, z_send, z_recv,
+    gs, gr, cs, cr, ts, tr, xs, xr, ns, nr, zs, zr,
 ):
     q = lax.axis_index("pole")
     place = lax.axis_index("row") * n_col + lax.axis_index("col")
@@ -126,14 +125,9 @@
 
         count = count + has_right.astype(jnp.int32) + has_left.astype(jnp.int32)
 
-    mixed[...] = jnp.zeros_like(mixed)
-    mixed[:, 0:share] = h_ref[0]
-    mixed[:, share : 2 * share] = o_ref[0]
-    mixed[:, 2 * share : 3 * share] = s_ref[0]
-    turned = mixed[...].T
     mine = pl.ds(pl.multiple_of(q * share, share), share)
-    for i in range(3):
-        gathered[mine, i * N : (i + 1) * N] = turned[i * share : (i + 1) * share]
+    for i, block in enumerate((h_ref, o_ref, s_ref)):
+        gathered[mine, i * N : (i + 1) * N] = block[0]
     pl.semaphore_wait(barrier, count)
     copies = []
     for o in range(1, n_pole):
@@ -176,11 +170,38 @@
         a = jnp.where(diag_mask, a, 0.0) + padding
         a_all[p] = a
         work[p] = a
+        d_all[p] = a
         f_all[p] = jnp.zeros((N, N), jnp.float32)
 
+    def exists(d):
+        return place + d < places, place >= d
+
+    def neighbour(d):
+        return at(jnp.minimum(place + d, places - 1)), at(jnp.maximum(place - d, 0))
+
+    def transfer(source, target, send, recv, d, side, slot):
+        return pltpu.make_async_remote_copy(
+            src_ref=source.at[(side, *slot)], dst_ref=target.at[(1 - side, *slot)],
+            send_sem=send.at[(side, *slot)], recv_sem=recv.at[(1 - side, *slot)],
+            device_id=neighbour(d)[side], device_id_type=MESH,
+        )
+
+    def start(copies, d):
+        for side, copy in copies:
+            pl.when(exists(d)[side])(copy.start)
+
+    def finish(copies, d, target, level):
+        for side in (0, 1):
+            @pl.when(jnp.logical_not(exists(d)[side]))
+            def _():
+                target[side, level] = jnp.zeros(target.shape[2:], jnp.float32)
+
+        for side, copy in copies:
+            pl.when(exists(d)[1 - side])(copy.wait_recv)
+            pl.when(exists(d)[side])(copy.wait_send)
+
+    crossing = None
     for level, d in enumerate(distances):
-        last = level == levels - 1
-        half = N if last else 2 * N
         invert(work, range(poles))
         if level == 0:
             @pl.when(has_left)
@@ -191,76 +212,42 @@
             def _():
                 link_t[...] = jnp.zeros_like(link_t)
 
+            link = link_t[...].T
             for p in range(poles):
                 ul[p, :N] = coupling_t[...]
-                ul[p, N:] = link_t[...].T
-        has_right_d = place + d < places
-        has_left_d = place >= d
-        rights, lefts = [], []
+                ul[p, N:] = link
+        else:
+            finish(crossing, distances[level - 1], n_recv, level - 1)
+            for p in range(poles):
+                ul[p, :N] = n_recv[0, level - 1, p]
+                ul[p, N:] = n_recv[1, level - 1, p]
+        products, terms = [], []
         for p in range(poles):
-            if level:
-                ul[p, :N] = recv_r[level - 1, p, :N]
-                ul[p, N:] = recv_l[level - 1, p, N:]
             both = ul[p]
             product = dot(both, work[p])
-            full = dot_t(product, both)
-            send_r[level, p] = full[:, :N]
-            send_l[level, p] = full[:, N:]
-            right = pltpu.make_async_remote_copy(
-                src_ref=send_r.at[level, p, pl.ds(0, half)],
-                dst_ref=recv_l.at[level, p, pl.ds(0, half)],
-                send_sem=rs.at[level, p], recv_sem=rr.at[level, p],
-                device_id=at(jnp.minimum(place + d, places - 1)), device_id_type=MESH,
-            )
-            low = 2 * N - half
-            left = pltpu.make_async_remote_copy(
-                src_ref=send_l.at[level, p, pl.ds(low, half)],
-                dst_ref=recv_r.at[level, p, pl.ds(low, half)],
-                send_sem=ls.at[level, p], recv_sem=lr.at[level, p],
-                device_id=at(jnp.maximum(place - d, 0)), device_id_type=MESH,
-            )
-            rights.append(right)
-            lefts.append(left)
-
-            @pl.when(has_right_d)
-            def _():
-                right.start()
-
-            @pl.when(has_left_d)
-            def _():
-                left.start()
-
-        @pl.when(jnp.logical_not(has_left_d))
-        def _():
-            recv_l[level] = jnp.zeros(recv_l.shape[1:], jnp.float32)
-
-        @pl.when(jnp.logical_not(has_right_d))
-        def _():
-            recv_r[level] = jnp.zeros(recv_r.shape[1:], jnp.float32)
-
+            products.append(product)
+            for side in (0, 1):
+                half = slice(side * N, (side + 1) * N)
+                t_send[side, level, p] = dot_t(product[half], both[half])
+                copy = transfer(t_send, t_recv, ts, tr, d, side, (level, p))
+                terms.append((side, copy))
+                start([(side, copy)], d)
+        crossing = []
+        if level < levels - 1:
+            for p in range(poles):
+                both = ul[p]
+                n_send[0, level, p] = dot_t(products[p][N:], both[:N])
+                n_send[1, level, p] = dot_t(products[p][:N], both[N:])
+                for side in (0, 1):
+                    copy = transfer(n_send, n_recv, xs, xr, d, side, (level, p))
+                    crossing.append((side, copy))
+                    start([(side, copy)], d)
+        finish(terms, d, t_recv, level)
         for p in range(poles):
-            @pl.when(has_left_d)
-            def _():
-                rights[p].wait_recv()
-
-            @pl.when(has_right_d)
-            def _():
-                lefts[p].wait_recv()
-
-            @pl.when(has_right_d)
-            def _():
-                rights[p].wait_send()
-
-            @pl.when(has_left_d)
-            def _():
-                lefts[p].wait_send()
-
-        for p in range(poles):
-            f_all[p] += recv_l[level, p, :N]
-            e = jnp.zeros((N, N), jnp.float32)
-            for earlier in range(level + 1):
-                e += recv_r[earlier, p, N:]
-            work[p] = a_all[p] - f_all[p] - e
+            f_all[p] += t_recv[1, level, p]
+            left = d_all[p] - (t_recv[0, level, p] + t_recv[1, level, p])
+            d_all[p] = left
+            work[p] = left
 
     @pl.when(has_right)
     def _():
@@ -320,11 +307,8 @@
     for o in range(1, n_pole):
         copies[o - 1].wait()
         result += z_recv[o - 1]
-    mixed[0:share] = result[:, :N]
-    mixed[share : 2 * share] = result[:, N:]
-    turned = mixed[...].T
-    diag_ref[0] = turned[:, :share]
-    off_ref[0] = turned[:, share : 2 * share]
+    diag_ref[0] = result[:, :N]
+    off_ref[0] = result[:, N:]
 
 
 def solution(mesh):
@@ -335,34 +319,36 @@
     def per_device(h_diag, h_off, s_diag, snode_size, col_order, shifts, weights):
         poles = shifts.shape[0]
         share = h_diag.shape[2]
+        h_diag, h_off, s_diag = (jnp.swapaxes(x, 1, 2) for x in (h_diag, h_off, s_diag))
         vmem = pl.BlockSpec(memory_space=pltpu.VMEM)
         smem = pl.BlockSpec(memory_space=pltpu.SMEM)
         f32 = functools.partial(lambda *shape: pltpu.VMEM(shape, jnp.float32))
         dma = pltpu.SemaphoreType.DMA
-        message = f32(levels, poles, 2 * N, N)
-        return tuple(
-            pl.pallas_call(
-                functools.partial(kernel, n_pole, n_col, places, poles, levels),
-                out_shape=[jax.ShapeDtypeStruct((1, N, share), jnp.float32)] * 2,
-                in_specs=[vmem, vmem, vmem, smem, vmem, smem, smem],
-                out_specs=[vmem, vmem],
-                scratch_shapes=[
-                    f32(N, N), f32(N, 3 * N), f32(N, N), f32(N, N), f32(poles, N, N),
-                    f32(2 * poles, N, N), f32(poles, N, N), f32(poles, 2 * N, N),
-                    message, message, message, message,
-                    f32(poles, N, N), f32(poles, N, N), f32(N, 2 * N),
-                    f32(n_pole - 1, share, 2 * N),
-                    dma((n_pole - 1,)), dma((n_pole - 1,)), dma, dma,
-                    dma((levels, poles)), dma((levels, poles)),
-                    dma((levels, poles)), dma((levels, poles)),
-                    dma, dma, dma((n_pole - 1,)), dma((n_pole - 1,)),
-                ],
-                compiler_params=pltpu.CompilerParams(
-                    collective_id=0, has_side_effects=True,
-                    vmem_limit_bytes=32 * 1024 * 1024,
-                ),
-            )(h_diag, h_off, s_diag, snode_size, col_order.reshape(1, N), shifts, weights)
-        )
+        crossings = max(levels - 1, 1)
+        results = pl.pallas_call(
+            functools.partial(kernel, n_pole, n_col, places, poles, levels),
+            out_shape=[jax.ShapeDtypeStruct((1, share, N), jnp.float32)] * 2,
+            in_specs=[vmem, vmem, vmem, smem, vmem, smem, smem],
+            out_specs=[vmem, vmem],
+            scratch_shapes=[
+                f32(N, 3 * N), f32(N, N), f32(N, N), f32(poles, N, N),
+                f32(2 * poles, N, N), f32(poles, N, N), f32(poles, N, N),
+                f32(poles, 2 * N, N),
+                f32(2, levels, poles, N, N), f32(2, levels, poles, N, N),
+                f32(2, crossings, poles, N, N), f32(2, crossings, poles, N, N),
+                f32(poles, N, N), f32(poles, N, N), f32(N, 2 * N),
+                f32(n_pole - 1, share, 2 * N),
+                dma((n_pole - 1,)), dma((n_pole - 1,)), dma, dma,
+                dma((2, levels, poles)), dma((2, levels, poles)),
+                dma((2, crossings, poles)), dma((2, crossings, poles)),
+                dma, dma, dma((n_pole - 1,)), dma((n_pole - 1,)),
+            ],
+            compiler_params=pltpu.CompilerParams(
+                collective_id=0, has_side_effects=True,
+                vmem_limit_bytes=32 * 1024 * 1024,
+            ),
+        )(h_diag, h_off, s_diag, snode_size, col_order.reshape(1, N), shifts, weights)
+        return tuple(jnp.swapaxes(x, 1, 2) for x in results)
 
     spread = P(("row", "col"), None, "pole")
     return jax.shard_map(

time: 78.8 us -> 72.2 us (0.916)
  Pallas kernels: 74.2 us -> 67.1 us
    pallas_call x1, Pallas kernels: 74.2 us -> 67.1 us  [per_device(): pl.pallas_call(functools.partial(kernel, n_pole, n_col, places, poles, le...]
    unnamed x15 -> x16, local copies, waits for them, and re-layouts: 2.23 us -> 4.03 us
    pallas_call x2 -> x0, local copies, waits for them, and re-layouts: 1.36 us -> none  [per_device(): pl.pallas_call(functools.partial(kernel, n_pole, n_col, places, poles, le...]
where the time goes in v3:
time: 72.2 us; the launch traced here: 71.8 us
  Pallas kernels  67.1 us (93%)
  local copies, waits for them, and re-layouts  4.03 us (6%)
    pallas_call x1, Pallas kernels, per_device(): pl.pallas_call(functools.partial(kernel, n_pole, n_col, places, poles, le...  67.1 us
    unnamed x16, local copies, waits for them, and re-layouts  4.03 us

profile of v3, /device:TPU:0, one launch (start us, length us, event | category | flops | bytes accessed | tf_op | source)
XLA Modules:
  0.0 71.8 jit_solution(15362112099656066030)
XLA Ops:
  0.6 0.0 copy-start.6
  0.6 0.0 copy-start.3
  0.7 0.0 copy-start.4
  0.7 0.0 copy-start.5
  0.7 0.6 copy-done.6
  1.3 0.0 copy-done.3
  1.3 0.0 copy-done.4
  1.3 0.0 copy-done.5
  1.3 0.0 copy-start
  1.3 0.7 copy-done
  2.1 0.0 copy-start.1
  2.1 0.7 copy-done.1
  2.8 0.0 copy-start.2
  2.8 0.7 copy-done.2
  3.5 67.1 %shard_map.86 = (f32[1,32,128]{2,1,0:T(8,128)S(1)}, f32[1,32,128]{2,1,0:T(8,128)S(1)}) custom-call(f32[1,32,128]{2,1,0:T(8,128)S(1)} %bitcast.6, f32[1,32,128]{2,1,0:T(8,128)S(1)} %bitcast.7, f32[1,32,128]{2,1,0:T(8,128)S(1)} %bitcast.8, s32[8]{0:T(128)S(1)} %copy-done.3, s32[1,128]{1,0:T(1,128)S(1)} %bitcast.11, f32[2]{0:T(128)S(1)} %copy-done.5, ...), custom_call_target="tpu_custom_call" | custom-call | tf_op jit(solution)/shard_map/pallas_call | solution.py:328
  70.5 0.6 copy.11
  71.2 0.6 copy.12
Async XLA Ops:
  0.6 0.7 copy-start.6
  0.6 0.7 copy-start.3
  0.7 0.7 copy-start.4
  0.7 0.7 copy-start.5
  1.3 0.7 copy-start
  2.1 0.7 copy-start.1
  2.8 0.7 copy-start.2

commit v4 on v3

--- a/solution.py
+++ b/solution.py
@@ -88,6 +88,30 @@
     lax.fori_loop(0, N // PANEL, step, 0)
 
 
+def pack(full):
+    row = lax.broadcasted_iota(jnp.int32, (N // 2, N), 0)
+    col = lax.broadcasted_iota(jnp.int32, (N // 2, N), 1)
+    top, bottom = full[: N // 2], full[N // 2 :]
+    body = jnp.where(row <= col, top, pltpu.roll(bottom, N // 2, 1))
+    diagonal = jnp.sum(jnp.where(col == row + N // 2, bottom, 0.0), axis=0, keepdims=True)
+    return body, jnp.broadcast_to(diagonal, (8, N))
+
+
+def unpack(packed):
+    row = lax.broadcasted_iota(jnp.int32, (N // 2, N), 0)
+    col = lax.broadcasted_iota(jnp.int32, (N // 2, N), 1)
+    body = packed[: N // 2]
+    diagonal = jnp.broadcast_to(packed[N // 2 : N // 2 + 1], (N // 2, N))
+    turned = jnp.concatenate([body, body], axis=0).T
+    high, low = turned[: N // 2], turned[N // 2 :]
+    top = jnp.where(row <= col, body, high)
+    corner = jnp.where(
+        col - N // 2 < row, pltpu.roll(body, N // 2, 1), pltpu.roll(high, N // 2, 1)
+    )
+    corner = jnp.where(col - N // 2 == row, diagonal, corner)
+    return jnp.concatenate([top, jnp.where(col < N // 2, low, corner)], axis=0)
+
+
 def kernel(
     n_pole, n_col, places, poles, levels,
     h_ref, o_ref, s_ref, size_ref, order_ref, shift_ref, weight_ref,
@@ -228,7 +252,9 @@
             products.append(product)
             for side in (0, 1):
                 half = slice(side * N, (side + 1) * N)
-                t_send[side, level, p] = dot_t(product[half], both[half])
+                body, diagonal = pack(dot_t(product[half], both[half]))
+                t_send[side, level, p, : N // 2] = body
+                t_send[side, level, p, N // 2 :] = diagonal
                 copy = transfer(t_send, t_recv, ts, tr, d, side, (level, p))
                 terms.append((side, copy))
                 start([(side, copy)], d)
@@ -244,8 +270,9 @@
                     start([(side, copy)], d)
         finish(terms, d, t_recv, level)
         for p in range(poles):
-            f_all[p] += t_recv[1, level, p]
-            left = d_all[p] - (t_recv[0, level, p] + t_recv[1, level, p])
+            before = unpack(t_recv[1, level, p])
+            f_all[p] += before
+            left = d_all[p] - (unpack(t_recv[0, level, p]) + before)
             d_all[p] = left
             work[p] = left
 
@@ -260,7 +287,9 @@
     total = jnp.zeros((N, N), jnp.float32)
     for p in range(poles):
         scaled = weight_ref[p] * work[p]
-        g_send[p] = scaled
+        body, diagonal = pack(scaled)
+        g_send[p, : N // 2] = body
+        g_send[p, N // 2 :] = diagonal
         total += scaled
     to_left = pltpu.make_async_remote_copy(
         src_ref=g_send, dst_ref=g_recv, send_sem=ns, recv_sem=nr,
@@ -285,7 +314,7 @@
 
     off_t = jnp.zeros((N, N), jnp.float32)
     for p in range(poles):
-        off_t -= dot(g_recv[p], halves[p])
+        off_t -= dot(unpack(g_recv[p]), halves[p])
     z_send[:, N:] = dot(order, jnp.where(link_mask_t, off_t, 0.0))
 
     copies = []
@@ -334,9 +363,9 @@
                 f32(N, 3 * N), f32(N, N), f32(N, N), f32(poles, N, N),
                 f32(2 * poles, N, N), f32(poles, N, N), f32(poles, N, N),
                 f32(poles, 2 * N, N),
-                f32(2, levels, poles, N, N), f32(2, levels, poles, N, N),
+                f32(2, levels, poles, 72, N), f32(2, levels, poles, 72, N),
                 f32(2, crossings, poles, N, N), f32(2, crossings, poles, N, N),
-                f32(poles, N, N), f32(poles, N, N), f32(N, 2 * N),
+                f32(poles, 72, N), f32(poles, 72, N), f32(N, 2 * N),
                 f32(n_pole - 1, share, 2 * N),
                 dma((n_pole - 1,)), dma((n_pole - 1,)), dma, dma,
                 dma((2, levels, poles)), dma((2, levels, poles)),

time: 72.2 us -> 67.6 us (0.936)
  Pallas kernels: 67.1 us -> 62.4 us
    pallas_call x1, Pallas kernels: 67.1 us -> 62.4 us  [per_device(): pl.pallas_call(functools.partial(kernel, n_pole, n_col, places, poles, le...]
where the time goes in v4:
time: 67.6 us; the launch traced here: 67.1 us
  Pallas kernels  62.4 us (92%)
  local copies, waits for them, and re-layouts  4.03 us (6%)
  between operations  0.68 us (1%)
    pallas_call x1, Pallas kernels, per_device(): pl.pallas_call(functools.partial(kernel, n_pole, n_col, places, poles, le...  62.4 us
    unnamed x16, local copies, waits for them, and re-layouts  4.03 us

profile of v4, /device:TPU:0, one launch (start us, length us, event | category | flops | bytes accessed | tf_op | source)
XLA Modules:
  0.0 67.1 jit_solution(11275261658134495165)
XLA Ops:
  0.6 0.0 copy-start.6
  0.6 0.0 copy-start.3
  0.7 0.0 copy-start.4
  0.7 0.0 copy-start.5
  0.7 0.6 copy-done.6
  1.3 0.0 copy-done.3
  1.3 0.0 copy-done.4
  1.3 0.0 copy-done.5
  1.3 0.0 copy-start
  1.3 0.7 %copy-done = f32[1,128,32]{1,2,0:T(8,128)S(1)} copy-done((f32[1,128,32]{1,2,0:T(8,128)S(1)}, f32[1,128,32]{1,2,0:T(8,128)}, u32[]{:S(2)}) %copy-start) | copy-done | bytes 16408
  2.1 0.0 copy-start.1
  2.1 0.7 %copy-done.1 = f32[1,128,32]{1,2,0:T(8,128)S(1)} copy-done((f32[1,128,32]{1,2,0:T(8,128)S(1)}, f32[1,128,32]{1,2,0:T(8,128)}, u32[]{:S(2)}) %copy-start.1) | copy-done | bytes 16408
  2.8 0.0 copy-start.2
  2.8 0.7 %copy-done.2 = f32[1,128,32]{1,2,0:T(8,128)S(1)} copy-done((f32[1,128,32]{1,2,0:T(8,128)S(1)}, f32[1,128,32]{1,2,0:T(8,128)}, u32[]{:S(2)}) %copy-start.2) | copy-done | bytes 16408
  3.5 62.4 %shard_map.86 = (f32[1,32,128]{2,1,0:T(8,128)S(1)}, f32[1,32,128]{2,1,0:T(8,128)S(1)}) custom-call(f32[1,32,128]{2,1,0:T(8,128)S(1)} %bitcast.6, f32[1,32,128]{2,1,0:T(8,128)S(1)} %bitcast.7, f32[1,32,128]{2,1,0:T(8,128)S(1)} %bitcast.8, s32[8]{0:T(128)S(1)} %copy-done.3, s32[1,128]{1,0:T(1,128)S(1)} %bitcast.11, f32[2]{0:T(128)S(1)} %copy-done.5, ...), custom_call_target="tpu_custom_call" | custom-call | tf_op jit(solution)/shard_map/pallas_call | solution.py:357
  65.9 0.6 copy.11
  66.5 0.6 copy.12
Async XLA Ops:
  0.6 0.7 copy-start.6
  0.6 0.7 copy-start.3
  0.7 0.7 copy-start.4
  0.7 0.7 %copy-start.5 = (f32[2]{0:T(128)S(1)}, f32[2]{0:T(128)}, u32[]{:S(2)}) copy-start(f32[2]{0:T(128)} %shift_ref.1) | copy-start | bytes 28
  1.3 0.7 %copy-start = (f32[1,128,32]{1,2,0:T(8,128)S(1)}, f32[1,128,32]{1,2,0:T(8,128)}, u32[]{:S(2)}) copy-start(f32[1,128,32]{1,2,0:T(8,128)} %param.7) | copy-start | bytes 49156
  2.1 0.7 %copy-start.1 = (f32[1,128,32]{1,2,0:T(8,128)S(1)}, f32[1,128,32]{1,2,0:T(8,128)}, u32[]{:S(2)}) copy-start(f32[1,128,32]{1,2,0:T(8,128)} %param.8) | copy-start | bytes 49156
  2.8 0.7 %copy-start.2 = (f32[1,128,32]{1,2,0:T(8,128)S(1)}, f32[1,128,32]{1,2,0:T(8,128)}, u32[]{:S(2)}) copy-start(f32[1,128,32]{1,2,0:T(8,128)} %param.9) | copy-start | bytes 49156
